TPU v7x, 32 devices: a whole 2x2x4 slice. The times are simulated.
32 devices in a mesh: dp: 4 (over z), sq: 8 (over y, x, core).
Axes of the slice: x: 2, y: 2, z: 4, core: 2. Of those that a mesh axis runs over, the one named last changes fastest.
Arguments:
- frames: bfloat16 [4, 1024, 1024], P('dp', 'sq'), may hold values from -6 to 6
- norm1_gain: float32 [1024], replicated, may hold values from 0.5 to 1.5
- w_qkv: bfloat16 [1024, 3072], replicated, may hold values from -0.1875 to 0.1875
- w_out: bfloat16 [1024, 1024], replicated, may hold values from -0.75 to 0.75
- norm2_gain: float32 [1024], replicated, may hold values from 0.5 to 1.5
- w_up: bfloat16 [1024, 4096], replicated, may hold values from -0.1875 to 0.1875
- w_down: bfloat16 [4096, 1024], replicated, may hold values from -0.09375 to 0.09375
- lengths: int32 [4, 8], P('dp'), may hold values from 1 to 896, as said below
- cotangent: bfloat16 [4, 1024, 1024], P('dp', 'sq'), may hold values from -6 to 6
Outputs:
- out: bfloat16 [4, 1024, 1024], P('dp', 'sq')
- d_in: float32 [4, 1024, 1024], P('dp', 'sq')
- g_norm1: float32 [1024], P('sq')
- g_qkv: float32 [1024, 3072], P('sq')
- g_out: float32 [1024, 1024], P('sq')
- g_norm2: float32 [1024], P('sq')
- g_up: float32 [1024, 4096], P('sq')
- g_down: float32 [4096, 1024], P('sq')
Inputs may be any that keep to these rules, and one draw needn't show every extreme that they name: Each row's lengths sum to 1024. In each row exactly one item has 896 frames and is neither the first nor the last item of the row; the other items share the remaining 128 frames.
All inputs are finite; a program needn't handle non-finite values.
Results may differ from a plain program's by a relative error of at most 0.025.
Values may be sent and summed in bfloat16 or wider, within the bound.
A program may use at most 256 MiB of HBM per device.

v0:
```python
import jax
import jax.numpy as jnp
from jax import lax
from jax.sharding import PartitionSpec as P

HEADS = 16
HEAD_DIM = 64
EPSILON = 1e-05
NEG_FILL = -1000000000.0
START_MAX = -1e30


def norm_scaled(values, gain):
    return values * lax.rsqrt(jnp.mean(values * values, axis=-1, keepdims=True) + EPSILON) * gain


def segment_ids(positions, item_ends):
    return jnp.sum((positions[None, :, None] >= item_ends[:, None, :]).astype(jnp.int32), axis=2)


def visible(query_pos, query_seg, key_pos, key_seg):
    return (key_pos[None, None, :] <= query_pos[None, :, None]) & (
        key_seg[:, None, :] == query_seg[:, :, None]
    )


def block_size(count, limit):
    for candidate in range(min(count, limit), 0, -1):
        if count % candidate == 0:
            return candidate
    return count


def over_blocks(carry, arrays, start, step_fn, limit):
    count = arrays[0].shape[1]
    size = block_size(count, limit)
    number = count // size
    if number == 1:
        return step_fn(carry, arrays, start)
    stacked = tuple(
        (
            jnp.swapaxes(member.reshape((member.shape[0], number, size) + member.shape[2:]), 0, 1)
            for member in arrays
        )
    )

    def turn(state, item):
        offset, pieces = item
        return (step_fn(state, pieces, start + offset * size), None)

    offsets = jnp.arange(number, dtype=jnp.int32)
    return lax.scan(turn, carry, (offsets, stacked))[0]


def contract_rows(left, right):
    return lax.dot_general(
        left, right, (((0,), (0,)), ((), ())), preferred_element_type=jnp.float32
    )


def times_transpose(left, right):
    return lax.dot_general(
        left, right, (((1,), (1,)), ((), ())), preferred_element_type=jnp.float32
    )


def heads_flat(values, batch, rows, width):
    return values.transpose(0, 2, 1, 3).reshape(batch * rows, width)


def shards(frames, norm1_gain, w_qkv, w_out, norm2_gain, w_up, w_down, lengths, cotangent):
    batch = frames.shape[0]
    rows = frames.shape[1]
    width = frames.shape[2]
    factor = HEAD_DIM ** (-0.5)
    first = lax.axis_index("sq") * rows
    query_pos = first + jnp.arange(rows, dtype=jnp.int32)
    item_ends = jnp.cumsum(lengths, axis=1)
    query_seg = segment_ids(query_pos, item_ends)
    frames_own = frames.reshape(batch * rows, width).astype(jnp.float32)
    hidden1, norm1_pull = jax.vjp(norm_scaled, frames_own, norm1_gain)
    hidden1_low = hidden1.astype(jnp.bfloat16)
    mixed = jnp.dot(hidden1_low, w_qkv, preferred_element_type=jnp.float32).astype(jnp.bfloat16)
    query_rows = mixed[:, :width].reshape(batch, rows, width)
    key_rows = mixed[:, width : 2 * width].reshape(batch, rows, width)
    value_rows = mixed[:, 2 * width :].reshape(batch, rows, width)
    queries = query_rows.reshape(batch, rows, HEADS, HEAD_DIM)
    keys_own = key_rows.reshape(batch, rows, HEADS, HEAD_DIM)
    values_own = value_rows.reshape(batch, rows, HEADS, HEAD_DIM)

    def forward_step(carry, pieces, start):
        key_piece, value_piece = pieces
        count = key_piece.shape[1]
        key_pos = start + jnp.arange(count, dtype=jnp.int32)
        key_seg = segment_ids(key_pos, item_ends)

        def forward_work(state):
            running_max, running_sum, accum = state
            keys_block = key_piece.reshape(batch, count, HEADS, HEAD_DIM)
            values_block = value_piece.reshape(batch, count, HEADS, HEAD_DIM)
            scores = (
                jnp.einsum(
                    "rqhd,rkhd->rhqk", queries, keys_block, preferred_element_type=jnp.float32
                )
                * factor
            )
            mask = visible(query_pos, query_seg, key_pos, key_seg)[:, None]
            scores = jnp.where(mask, scores, NEG_FILL)
            new_max = jnp.maximum(running_max, jnp.max(scores, axis=-1))
            weights = jnp.where(mask, jnp.exp(scores - new_max[..., None]), 0.0)
            decay = jnp.exp(running_max - new_max)
            new_sum = decay * running_sum + jnp.sum(weights, axis=-1)
            update = jnp.einsum(
                "rhqk,rkhd->rhqd",
                weights.astype(jnp.bfloat16),
                values_block,
                preferred_element_type=jnp.float32,
            )
            return (new_max, new_sum, decay[..., None] * accum + update)

        return lax.cond(start <= query_pos[-1], forward_work, lambda state: state, carry)

    start_state = (
        jnp.full((batch, HEADS, rows), START_MAX, jnp.float32),
        jnp.zeros((batch, HEADS, rows), jnp.float32),
        jnp.zeros((batch, HEADS, rows, HEAD_DIM), jnp.float32),
    )
    final_max, final_sum, accum = over_blocks(
        start_state,
        (
            lax.all_gather(key_rows, "sq", axis=1, tiled=True),
            lax.all_gather(value_rows, "sq", axis=1, tiled=True),
        ),
        jnp.int32(0),
        forward_step,
        512,
    )
    attended = heads_flat(accum / final_sum[..., None], batch, rows, width)
    log_total = final_max + jnp.log(final_sum)
    attended_low = attended.astype(jnp.bfloat16)
    middle = frames_own + jnp.dot(attended_low, w_out, preferred_element_type=jnp.float32)
    hidden2, norm2_pull = jax.vjp(norm_scaled, middle, norm2_gain)
    hidden2_low = hidden2.astype(jnp.bfloat16)
    upward = jnp.dot(hidden2_low, w_up, preferred_element_type=jnp.float32)
    active, gelu_pull = jax.vjp(jax.nn.gelu, upward)
    active_low = active.astype(jnp.bfloat16)
    result = middle + jnp.dot(active_low, w_down, preferred_element_type=jnp.float32)
    grad_top = cotangent.reshape(batch * rows, width).astype(jnp.float32)
    grad_branch = grad_top.astype(jnp.bfloat16)
    grad_down = contract_rows(active_low, grad_branch)
    grad_active = times_transpose(grad_branch, w_down)
    grad_upward = gelu_pull(grad_active)[0].astype(jnp.bfloat16)
    grad_up = contract_rows(hidden2_low, grad_upward)
    grad_hidden2 = times_transpose(grad_upward, w_up)
    grad_middle_part, grad_gain2 = norm2_pull(grad_hidden2)
    grad_middle = grad_top + grad_middle_part
    grad_attn = grad_middle.astype(jnp.bfloat16)
    grad_outproj = contract_rows(attended_low, grad_attn)
    grad_attended = times_transpose(grad_attn, w_out).astype(jnp.bfloat16)
    grad_rows_own = grad_attended.reshape(batch, rows, width)
    grad_heads = grad_attended.reshape(batch, rows, HEADS, HEAD_DIM)
    delta_rows = jnp.sum(
        (grad_attended.astype(jnp.float32) * attended).reshape(batch, rows, HEADS, HEAD_DIM), axis=3
    )
    delta = delta_rows.transpose(0, 2, 1)

    def query_step(carry, pieces, start):
        key_piece, value_piece = pieces
        count = key_piece.shape[1]
        key_pos = start + jnp.arange(count, dtype=jnp.int32)
        key_seg = segment_ids(key_pos, item_ends)

        def query_work(grad_query):
            keys_block = key_piece.reshape(batch, count, HEADS, HEAD_DIM)
            values_block = value_piece.reshape(batch, count, HEADS, HEAD_DIM)
            scores = (
                jnp.einsum(
                    "rqhd,rkhd->rhqk", queries, keys_block, preferred_element_type=jnp.float32
                )
                * factor
            )
            mask = visible(query_pos, query_seg, key_pos, key_seg)[:, None]
            shares = jnp.where(mask, jnp.exp(scores - log_total[..., None]), 0.0)
            grad_shares = jnp.einsum(
                "rqhd,rkhd->rhqk", grad_heads, values_block, preferred_element_type=jnp.float32
            )
            grad_scores = (shares * (grad_shares - delta[..., None])).astype(jnp.bfloat16)
            return grad_query + jnp.einsum(
                "rhqk,rkhd->rhqd", grad_scores, keys_block, preferred_element_type=jnp.float32
            )

        return lax.cond(start <= query_pos[-1], query_work, lambda state: state, carry)

    zero_query = jnp.zeros((batch, HEADS, rows, HEAD_DIM), jnp.float32)
    grad_query = over_blocks(
        zero_query,
        (
            lax.all_gather(key_rows, "sq", axis=1, tiled=True),
            lax.all_gather(value_rows, "sq", axis=1, tiled=True),
        ),
        jnp.int32(0),
        query_step,
        512,
    )

    def key_step(carry, pieces, start):
        query_piece, grad_piece, total_piece, delta_piece = pieces
        count = query_piece.shape[1]
        remote_pos = start + jnp.arange(count, dtype=jnp.int32)
        remote_seg = segment_ids(remote_pos, item_ends)

        def key_work(state):
            grad_key, grad_value = state
            remote_queries = query_piece.reshape(batch, count, HEADS, HEAD_DIM)
            remote_grads = grad_piece.reshape(batch, count, HEADS, HEAD_DIM)
            scores = (
                jnp.einsum(
                    "rqhd,rkhd->rhqk", remote_queries, keys_own, preferred_element_type=jnp.float32
                )
                * factor
            )
            mask = visible(remote_pos, remote_seg, query_pos, query_seg)[:, None]
            shares = jnp.where(
                mask, jnp.exp(scores - total_piece.transpose(0, 2, 1)[..., None]), 0.0
            )
            grad_value = grad_value + jnp.einsum(
                "rhqk,rqhd->rhkd",
                shares.astype(jnp.bfloat16),
                remote_grads,
                preferred_element_type=jnp.float32,
            )
            grad_shares = jnp.einsum(
                "rqhd,rkhd->rhqk", remote_grads, values_own, preferred_element_type=jnp.float32
            )
            grad_scores = (
                shares * (grad_shares - delta_piece.transpose(0, 2, 1)[..., None])
            ).astype(jnp.bfloat16)
            grad_key = grad_key + jnp.einsum(
                "rhqk,rqhd->rhkd", grad_scores, remote_queries, preferred_element_type=jnp.float32
            )
            return (grad_key, grad_value)

        return lax.cond(start + count - 1 >= first, key_work, lambda state: state, carry)

    grad_key, grad_value = over_blocks(
        (zero_query, zero_query),
        (
            lax.all_gather(query_rows, "sq", axis=1, tiled=True),
            lax.all_gather(grad_rows_own, "sq", axis=1, tiled=True),
            lax.all_gather(
                log_total.transpose(0, 2, 1).astype(jnp.bfloat16), "sq", axis=1, tiled=True
            ).astype(jnp.float32),
            lax.all_gather(delta_rows.astype(jnp.bfloat16), "sq", axis=1, tiled=True).astype(
                jnp.float32
            ),
        ),
        jnp.int32(0),
        key_step,
        512,
    )
    grad_mixed = jnp.concatenate(
        [
            heads_flat(grad_query * factor, batch, rows, width),
            heads_flat(grad_key * factor, batch, rows, width),
            heads_flat(grad_value, batch, rows, width),
        ],
        axis=1,
    ).astype(jnp.bfloat16)
    grad_qkv = contract_rows(hidden1_low, grad_mixed)
    grad_hidden1 = times_transpose(grad_mixed, w_qkv)
    grad_frames_part, grad_gain1 = norm1_pull(grad_hidden1)
    grad_frames = (grad_middle + grad_frames_part).reshape(batch, rows, width)
    result_rows = result.astype(jnp.bfloat16).reshape(batch, rows, width)
    shares_sq = (
        lax.psum_scatter(grad_gain1, "sq", scatter_dimension=0, tiled=True),
        lax.psum_scatter(grad_qkv, "sq", scatter_dimension=0, tiled=True),
        lax.psum_scatter(grad_outproj, "sq", scatter_dimension=0, tiled=True),
        lax.psum_scatter(grad_gain2, "sq", scatter_dimension=0, tiled=True),
        lax.psum_scatter(grad_up, "sq", scatter_dimension=0, tiled=True),
        lax.psum_scatter(grad_down, "sq", scatter_dimension=0, tiled=True),
    )
    totals = (
        lax.psum(shares_sq[0].astype(jnp.bfloat16), "dp").astype(jnp.float32),
        lax.psum(shares_sq[1].astype(jnp.bfloat16), "dp").astype(jnp.float32),
        lax.psum(shares_sq[2].astype(jnp.bfloat16), "dp").astype(jnp.float32),
        lax.psum(shares_sq[3].astype(jnp.bfloat16), "dp").astype(jnp.float32),
        lax.psum(shares_sq[4].astype(jnp.bfloat16), "dp").astype(jnp.float32),
        lax.psum(shares_sq[5].astype(jnp.bfloat16), "dp").astype(jnp.float32),
    )
    return (
        result_rows,
        grad_frames,
        totals[0],
        totals[1],
        totals[2],
        totals[3],
        totals[4],
        totals[5],
    )


def solution(mesh):
    return jax.shard_map(
        shards,
        mesh=mesh,
        in_specs=(
            P("dp", "sq", None),
            P(),
            P(),
            P(),
            P(),
            P(),
            P(),
            P("dp", None),
            P("dp", "sq", None),
        ),
        out_specs=(
            P("dp", "sq", None),
            P("dp", "sq", None),
            P("sq"),
            P("sq", None),
            P("sq", None),
            P("sq"),
            P("sq", None),
            P("sq", None),
        ),
        check_vma=False,
    )
```

profile of v0, /device:TPU:0, one launch (start us, length us, event | category | flops | bytes accessed | tf_op | source)
XLA Modules:
  0.0 698.9 jit_solution(101815978232163255)
XLA Ops:
  9.0 4.0 convolution_convert_fusion
  18.7 26.0 %all-gather.9.cloned.1.call-done = bf16[1024,1024]{1,0:T(8,128)(2,1)} async-done(((bf16[128,1024]{1,0:T(8,128)(2,1)}), bf16[1024,1024]{1,0:T(8,128)(2,1)}) %all-gather.9.cloned.1.call-update) | async-done | bytes 2097168 | tf_op jit(solution)/shard_map/all_gather | solution.py:131
  48.6 26.5 %all-gather.11.cloned.1.call-done = bf16[1024,1024]{1,0:T(8,128)(2,1)} async-done(((bf16[128,1024]{1,0:T(8,128)(2,1)}), bf16[1024,1024]{1,0:T(8,128)(2,1)}) %all-gather.11.cloned.1.call-update) | async-done | bytes 2097168 | tf_op jit(solution)/shard_map/all_gather | solution.py:132
  79.1 13.9 %while.45 = (s32[]{:T(128)}, f32[1,16,128]{2,1,0:T(8,128)S(1)}, f32[1,16,128]{2,1,0:T(8,128)S(1)}, f32[1,16,128,64]{2,3,1,0:T(8,128)S(1)}, s32[2]{0:T(128)S(1)},...) while((s32[]{:T(128)}, f32[1,16,128]{2,1,0:T(8,128)S(1)}, ...), condition=%wide.region_9.10_spmd, body=%wide.region_3.9_spmd.sunk | while | flops 282544640 | bytes 20628860 | solution.py:52
  83.0 6.1 conditional.8
  98.3 4.9 fusion.92
  103.2 7.7 %fusion.60 = bf16[128,4096]{1,0:T(8,128)(2,1)S(1)} fusion(f32[128,4096]{1,0:T(8,128)S(1)} %fusion.92, bf16[4096,1024]{1,0:T(8,128)(2,1)} %param.27, bf16[1,128,1024]{2,1,0:T(8,128)(2,1)S(1)} %copy-done.18), kind=kOutput, calls=%fused_computation.80 | convolution fusion | flops 1084227584 | bytes 11796480 | tf_op jit(solution)/shard_map/dot_general | solution.py:62
  124.1 4.0 copy.73
  129.7 15.0 %all_gather.25 = bf16[1,1024,16]{1,2,0:T(8,128)(2,1)S(1)} all-gather(bf16[1,128,16]{1,2,0:T(8,128)(2,1)S(1)} %bitcast_convert_fusion), channel_id=1, replica_groups=mesh['dp'=4,'sq'=8] {'sq'}, dimensions={1}, use_global_device_ids=true | all-gather | bytes 36864 | tf_op jit(solution)/shard_map/all_gather | solution.py:253
  145.3 8.0 %all_gather.23 = bf16[1,1024,16]{1,2,0:T(8,128)(2,1)S(1)} all-gather(bf16[1,128,16]{1,2,0:T(8,128)(2,1)S(1)} %get-tuple-element.1073), channel_id=1, replica_groups=mesh['dp'=4,'sq'=8] {'sq'}, dimensions={1}, use_global_device_ids=true | all-gather | bytes 36864 | tf_op jit(solution)/shard_map/all_gather | solution.py:250
  155.3 20.4 %while.46 = (s32[]{:T(128)}, f32[1,16,128,64]{2,3,1,0:T(8,128)}, s32[2]{0:T(128)}, s32[128]{0:T(128)}, s32[1,8]{1,0:T(1,128)}, /*index=5*/s32[1,128]{1,0:T(1,128...) while((s32[]{:T(128)}, f32[1,16,128,64]{2,3,1,0:T(8,128)}, ...), condition=%wide.region_17.18_spmd, body=%wide.region_13.17_spmd.sunk | while | flops 409285120 | bytes 17499484 | solution.py:52
  159.7 11.6 %conditional.9 = (f32[1,16,128,64]{2,3,1,0:T(8,128)}) conditional(s32[]{:T(128)} %convert_element_type.291, f32[1,16,128,64]{2,3,1,0:T(8,128)} %get-tuple-element.1437, (s32[]{:T(128)}, s32[512]{0:T(512)S(1)}, s32[128]{0:T(128)}, s32[1,512,8]{1,2,0:T(8,128)S(1)}, s32[1,128]{1,0:T(1,128)}, /*index=5*/bf16[2,1,512,1024]{2,3,1,0:T(8,128)(2,1)}, ...), branch_computations={%region_14.14_spmd, %region_15.16_spmd} | conditional | flops 409276416 | bytes 17476628 | solution.py:192
  165.8 5.5 fusion.23
  177.5 4.0 copy.75
  182.4 36.2 %while.47 = (s32[]{:T(128)}, f32[1,16,128,64]{2,3,1,0:T(8,128)S(1)}, f32[1,16,128,64]{2,3,1,0:T(8,128)}, s32[2]{0:T(128)S(1)}, s32[]{:T(128)}, /*index=5*/s32[1,...) while((s32[]{:T(128)}, ...), condition=%wide.region_22.23_spmd.clone.clone, body=%wide.region_18.22_spmd.clone.clone.sunk | while | flops 547828352 | bytes 28265440 | solution.py:52
  184.5 16.3 %conditional.10 = ((f32[1,16,128,64]{2,3,1,0:T(8,128)S(1)}, f32[1,16,128,64]{2,3,1,0:T(8,128)})) conditional(s32[]{:T(128)} %convert_element_type.293, (f32[1,16,128,64]{2,3,1,0:T(8,128)S(1)}, f32[1,16,128,64]{2,3,1,0:T(8,128)}) %tuple.150, (s32[]{:T(128)}, s32[]{:T(128)}, s32[512]{0:T(512)S(1)}, s32[1,128]{1,0:T(1,128)S(1)}, ...), branch_computations={%region_19.19_spmd, %region_20.21_spmd} | conditional | flops 547819648 | bytes 28242020 | solution.py:243
  190.0 6.2 fusion.42
  196.2 4.5 fusion.43
  202.8 15.9 %conditional.10 = ((f32[1,16,128,64]{2,3,1,0:T(8,128)S(1)}, f32[1,16,128,64]{2,3,1,0:T(8,128)})) conditional(s32[]{:T(128)} %convert_element_type.293, (f32[1,16,128,64]{2,3,1,0:T(8,128)S(1)}, f32[1,16,128,64]{2,3,1,0:T(8,128)}) %tuple.150, (s32[]{:T(128)}, s32[]{:T(128)}, s32[512]{0:T(512)S(1)}, s32[1,128]{1,0:T(1,128)S(1)}, ...), branch_computations={%region_19.19_spmd, %region_20.21_spmd} | conditional | flops 547819648 | bytes 28242020 | solution.py:243
  208.3 6.2 fusion.42
  214.4 4.2 fusion.43
  219.8 7.5 %fusion.72 = f32[1024,3072]{1,0:T(8,128)} fusion(bf16[128,1024]{0,1:T(8,128)(2,1)S(1)} %bitcast.228, bf16[128,1024]{0,1:T(8,128)(2,1)S(1)} %bitcast.230, bf16[128,1024]{0,1:T(8,128)(2,1)} %bitcast.226, bf16[1,128,1024]{2,1,0:T(8,128)(2,1)S(1)} %copy-done.4, f32[1024]{0:T(1024)S(1)} %copy-done.30, f32[128]{0:T(128)S(1)} %copy-done.38), kind=kOutput, calls=%fused_computation.111 | convolution fusion | flops 808189952 | bytes 13636096 | tf_op jit(solution)/shard_map/dot_general | solution.py:56
  228.5 11.2 %fusion.91 = f32[1024,4096]{1,0:T(8,128)} fusion(bf16[128,4096]{1,0:T(8,128)(2,1)S(1)} %copy-done.9, f32[128,1024]{1,0:T(8,128)S(1)} %get-tuple-element.1089, f32[1024]{0:T(1024)S(1)} %copy-done.29, f32[128]{0:T(128)S(1)} %copy-done.35), kind=kOutput, calls=%fused_computation.140 | convolution fusion | flops 1074135040 | bytes 18354688 | tf_op jit(solution)/shard_map/dot_general | solution.py:56
  241.9 8.9 %fusion.74 = f32[4096,1024]{1,0:T(8,128)} fusion(bf16[1,128,1024]{2,1,0:T(8,128)(2,1)S(1)} %copy-done.19, f32[128,4096]{1,0:T(8,128)S(1)} %copy-done.3), kind=kOutput, calls=%fused_computation.113 | convolution fusion | flops 1078460416 | bytes 19136512 | tf_op jit(solution)/shard_map/dot_general | solution.py:56
  252.8 67.5 %reduce-scatter.5.cloned.1.call-done = f32[128,3072]{1,0:T(8,128)} async-done(((f32[1024,3072]{1,0:T(8,128)}), f32[128,3072]{1,0:T(8,128)}) %reduce-scatter.5.cloned.1.call-update) | async-done | bytes 1572880 | tf_op jit(solution)/shard_map/reduce_scatter | solution.py:276
  322.6 117.6 %reduce-scatter.9.cloned.1.call-done = f32[128,4096]{1,0:T(8,128)} async-done(((f32[1024,4096]{1,0:T(8,128)}), f32[128,4096]{1,0:T(8,128)}) %reduce-scatter.9.cloned.1.call-update) | async-done | bytes 2097168 | tf_op jit(solution)/shard_map/reduce_scatter | solution.py:279
  442.9 117.3 %reduce-scatter.11.cloned.1.call-done = f32[512,1024]{1,0:T(8,128)} async-done(((f32[4096,1024]{1,0:T(8,128)}), f32[512,1024]{1,0:T(8,128)}) %reduce-scatter.11.cloned.1.call-update) | async-done | bytes 2097168 | tf_op jit(solution)/shard_map/reduce_scatter | solution.py:280
  564.8 5.7 fusion.62
  570.6 5.2 fusion.66
  575.8 13.8 %all-reduce.2 = (bf16[1024]{0:T(1024)(128)(2,1)S(1)}, bf16[1024]{0:T(1024)(128)(2,1)S(1)}) all-reduce(f32[1024]{0:T(1024)S(1)} %get-tuple-element.989, f32[1024]{0:T(1024)S(1)} %copy-done.36), channel_id=6, replica_groups=mesh['dp'=4,'sq'=8] {'sq'}, use_global_device_ids=true, to_apply=%region_25.26.clone | all-reduce | flops 2048 | bytes 12288
  589.8 12.4 %all-reduce.3 = (bf16[128]{0:T(256)(128)(2,1)S(1)}, bf16[128]{0:T(256)(128)(2,1)S(1)}) all-reduce(bf16[128]{0:T(256)(128)(2,1)S(1)} %dynamic-slice.7, bf16[128]{0:T(256)(128)(2,1)S(1)} %dynamic-slice.6), channel_id=1, replica_groups=mesh['dp'=4,'sq'=8] {'dp'}, use_global_device_ids=true, to_apply=%region_26.27 | all-reduce | flops 256 | bytes 1024 | tf_op jit(solution)/shard_map/psum | solution.py:283
  604.2 81.7 %all-reduce.7.cloned.1.call-done = (bf16[128,3072]{1,0:T(8,128)(2,1)}, bf16[128,1024]{1,0:T(8,128)(2,1)}, bf16[128,4096]{1,0:T(8,128)(2,1)}, bf16[512,1024]{1,0:T(8,128)(2,1)}) async-done(((bf16[128,3072]{1,0:T(8,128)(2,1)}, bf16[128,1024]{1,0:T(8,128)(2,1)}, bf16[128,4096]{1,0:T(8,128)(2,1)}, bf16[512,1024]{1,0:T(8,128)(2,1)}), (bf16[128,3072]{1,0:T(8,128)(2,1)}, bf16[128,1024]{1,0:T(8,128)(2,1)}, ...) | async-done | bytes 3145744 | tf_op jit(solution)/shard_map/psum | solution.py:284
  (234 shorter events, 101.9 us)
Async XLA Ops:
  7.2 89.5 %copy-start = (bf16[1024,1024]{1,0:T(8,128)(2,1)S(1)}, bf16[1024,1024]{1,0:T(8,128)(2,1)}, u32[]{:S(2)}) copy-start(bf16[1024,1024]{1,0:T(8,128)(2,1)} %param.24) | copy-start | bytes 6291460
  7.2 37.5 %all-gather.9.cloned.1.call-start = ((), (), s32[]{:S(2)}) async-start(), calls=%async_computation.8 | async-start | bytes 2359296 | tf_op jit(solution)/shard_map/all_gather | solution.py:131
  13.0 4.1 copy-start.42
  14.0 61.1 %all-gather.11.cloned.1.call-start = ((), (), s32[]{:S(2)}) async-start(), calls=%async_computation.9 | async-start | bytes 2359296 | tf_op jit(solution)/shard_map/all_gather | solution.py:132
  14.7 109.4 %all-gather.13.cloned.1.call-start = ((), (), s32[]{:S(2)}) async-start(), calls=%async_computation.10 | async-start | bytes 2359296 | tf_op jit(solution)/shard_map/all_gather | solution.py:248
  15.4 162.1 %all-gather.15.cloned.1.call-start = ((), (), s32[]{:S(2)}) async-start(), calls=%async_computation.11 | async-start | bytes 2359296 | tf_op jit(solution)/shard_map/all_gather | solution.py:249
  92.9 5.3 copy-start.32
  98.2 16.3 %copy-start.34 = (f32[128]{0:T(128)}, f32[128]{0:T(128)S(1)}, u32[]{:S(2)}) copy-start(f32[128]{0:T(128)S(1)} %fusion.88) | copy-start | bytes 1540
  98.3 4.9 copy-start.18
  98.3 12.7 %slice-start = ((s8[8388608]{0:T(1024)(128)(4,1)}), s8[4194304]{0:T(1024)(128)(4,1)S(1)}, s32[]{:S(2)}) async-start(s8[8388608]{0:T(1024)(128)(4,1)} %bitcast.209), calls=%async_computation.13 | async-start | bytes 8388608
  103.2 7.8 %copy-start.2 = (f32[128,4096]{1,0:T(8,128)}, f32[128,4096]{1,0:T(8,128)S(1)}, u32[]{:S(2)}) copy-start(f32[128,4096]{1,0:T(8,128)S(1)} %fusion.92) | copy-start | bytes 6291460
  103.2 7.8 %slice-start.1 = ((s8[8388608]{0:T(1024)(128)(4,1)}), s8[4194304]{0:T(1024)(128)(4,1)S(1)}, s32[]{:S(2)}) async-start(s8[8388608]{0:T(1024)(128)(4,1)} %bitcast.209), calls=%async_computation.14 | async-start | bytes 8388608
  117.3 133.6 %reduce-scatter.7.cloned.1.call-start = ((), (), s32[]{:S(2)}) async-start(), calls=%async_computation.5 | async-start | bytes 4718592 | tf_op jit(solution)/shard_map/reduce_scatter | solution.py:277
  121.3 198.9 %reduce-scatter.5.cloned.1.call-start = ((), (), s32[]{:S(2)}) async-start(), calls=%async_computation.4 | async-start | bytes 14155776 | tf_op jit(solution)/shard_map/reduce_scatter | solution.py:276
  177.5 4.9 copy-start.27
  177.5 4.9 copy-start.33
  182.4 37.4 %copy-start.30 = (f32[1024]{0:T(1024)S(1)}, f32[1024]{0:T(1024)}, u32[]{:S(2)}) copy-start(f32[1024]{0:T(1024)} %param.22) | copy-start | bytes 12292
  182.4 37.4 %copy-start.38 = (f32[128]{0:T(128)S(1)}, f32[128]{0:T(128)}, u32[]{:S(2)}) copy-start(f32[128]{0:T(128)} %copy-done.37) | copy-start | bytes 1540
  196.2 4.5 copy-start.16
  214.4 4.2 copy-start.16
  219.7 7.6 %copy-start.23 = (bf16[1,16,128,64]{2,3,1,0:T(8,128)(2,1)}, bf16[1,16,128,64]{2,3,1,0:T(8,128)(2,1)S(1)}, u32[]{:S(2)}) copy-start(bf16[1,16,128,64]{2,3,1,0:T(8,128)(2,1)S(1)} %convert.20) | copy-start | bytes 786436
  219.8 7.5 %copy-start.25 = (bf16[1,16,128,64]{2,3,1,0:T(8,128)(2,1)}, bf16[1,16,128,64]{2,3,1,0:T(8,128)(2,1)S(1)}, u32[]{:S(2)}) copy-start(bf16[1,16,128,64]{2,3,1,0:T(8,128)(2,1)S(1)} %multiply_convert_fusion.2) | copy-start | bytes 786436
  227.3 212.8 %reduce-scatter.9.cloned.1.call-start = ((), (), s32[]{:S(2)}) async-start(), calls=%async_computation.6 | async-start | bytes 18874368 | tf_op jit(solution)/shard_map/reduce_scatter | solution.py:279
  239.7 320.4 %reduce-scatter.11.cloned.1.call-start = ((), (), s32[]{:S(2)}) async-start(), calls=%async_computation.7 | async-start | bytes 18874368 | tf_op jit(solution)/shard_map/reduce_scatter | solution.py:280
  250.9 435.0 %all-reduce.7.cloned.1.call-start = ((), (), s32[]{:S(2)}) async-start(), calls=%async_computation.12 | async-start | bytes 6291456 | tf_op jit(solution)/shard_map/psum | solution.py:284
  564.8 5.8 copy-start.22
  564.8 5.8 copy-start.24
  564.8 5.8 copy-start.26
  564.8 5.8 copy-start.39
  570.6 5.2 copy-start.36
  570.6 32.6 %copy-start.41 = (f32[128]{0:T(128)S(1)}, f32[128]{0:T(128)}, u32[]{:S(2)}) copy-start(f32[128]{0:T(128)} %copy-done.40) | copy-start | bytes 1540
  570.6 32.6 %copy-start.6 = (f32[128,1024]{1,0:T(8,128)S(1)}, f32[128,1024]{1,0:T(8,128)}, u32[]{:S(2)}) copy-start(f32[128,1024]{1,0:T(8,128)} %copy-done.5) | copy-start | bytes 1572868
  (25 other events, 47.7 us)
Sparse Core Ops, SparseCore 0:
  14.1 30.5 all-gather.8
  47.2 27.8 all-gather.10
  77.0 27.8 all-gather.12
  117.5 34.1 all-gather.14
  154.8 51.3 reduce-scatter.6
  227.5 92.7 reduce-scatter.4
  324.2 115.9 reduce-scatter.8
  444.2 115.9 reduce-scatter.10
  563.5 122.3 all-reduce.6
where the time goes:
time: 700 us; the launch traced here: 699 us
  waiting for transfers between devices  438 us (63%)
  matrix products  103 us (15%)
  local copies, waits for them, and re-layouts  50.6 us (7%)
  blocking collectives  49.2 us (7%)
  other arithmetic  35.8 us (5%)
  between operations  15 us (2%)
    reduce_scatter x1, waiting for transfers between devices, shards(): lax.psum_scatter(grad_up, 'sq', scatter_dimension=0, tiled=True)  118 us
    reduce_scatter x1, waiting for transfers between devices, shards(): lax.psum_scatter(grad_down, 'sq', scatter_dimension=0, tiled=True)  117 us
    psum x1, waiting for transfers between devices, shards(): lax.psum(shares_sq[1].astype(jnp.bfloat16), 'dp').astype(jnp.float32)  81.7 us
    reduce_scatter x1, waiting for transfers between devices, shards(): lax.psum_scatter(grad_qkv, 'sq', scatter_dimension=0, tiled=True)  67.5 us
    dot_general x4, matrix products, contract_rows(): lax.dot_general(left, right, (((0,), (0,)), ((), ())), preferred_element_...  31.4 us
    all_gather x1, waiting for transfers between devices, shards(): lax.all_gather(value_rows, 'sq', axis=1, tiled=True)  26.5 us
    all_gather x1, waiting for transfers between devices, shards(): lax.all_gather(key_rows, 'sq', axis=1, tiled=True)  26 us
    dot_general x4, matrix products, times_transpose(): lax.dot_general(left, right, (((1,), (1,)), ((), ())), preferred_element_...  18.2 us
  transfers between devices with their start and end apart: 9, of which 6 were waited for; matrix products, arithmetic and copies ran while one was open for 24% of the time, Pallas kernels for 0%

commit v1 on v0

--- a/solution.py
+++ b/solution.py
@@ -8,6 +8,17 @@
 EPSILON = 1e-05
 NEG_FILL = -1000000000.0
 START_MAX = -1e30
+
+
+def collect(x, axis, dim):
+    ways = lax.axis_size(axis)
+    pieces = [x]
+    for far in range(1, ways):
+        pieces.append(
+            lax.ppermute(pieces[far - 1], axis, [(d, (d - 1) % ways) for d in range(ways)])
+        )
+    line = jnp.concatenate(pieces, axis=dim)
+    return jnp.roll(line, lax.axis_index(axis) * x.shape[dim], axis=dim)
 
 
 def norm_scaled(values, gain):
@@ -127,10 +138,7 @@
     )
     final_max, final_sum, accum = over_blocks(
         start_state,
-        (
-            lax.all_gather(key_rows, "sq", axis=1, tiled=True),
-            lax.all_gather(value_rows, "sq", axis=1, tiled=True),
-        ),
+        (lax.all_gather(key_rows, "sq", axis=1, tiled=True), collect(value_rows, "sq", 1)),
         jnp.int32(0),
         forward_step,
         512,

time: 700 us -> 714 us (1.020)
  waiting for transfers between devices: 438 us -> 410 us
  starting transfers between devices: 0.63 us -> 21 us
  local copies, waits for them, and re-layouts: 50.6 us -> 61.4 us
    all_gather x1, waiting for transfers between devices: 26.5 us -> 0.01 us  [shards(): lax.all_gather(value_rows, 'sq', axis=1, tiled=True)]
    all_gather x1, waiting for transfers between devices: 26 us -> 0.01 us  [shards(): lax.all_gather(key_rows, 'sq', axis=1, tiled=True)]
    ppermute x0 -> x7, waiting for transfers between devices: none -> 24.7 us  [collect(): lax.ppermute(pieces[far - 1], axis, [(d, (d - 1) % ways) for d in range(w...]
    ppermute x0 -> x7, starting transfers between devices: none -> 20.4 us  [collect(): lax.ppermute(pieces[far - 1], axis, [(d, (d - 1) % ways) for d in range(w...]
    unnamed x94 -> x109, local copies, waits for them, and re-layouts: 17.1 us -> 22.1 us
  transfers between devices with their start and end apart: 9 -> 16, of which waited for: 6 -> 11; matrix products, arithmetic and copies ran while one was open for 24% -> 25% of each run, Pallas kernels for 0% -> 0%
where the time goes in v1:
time: 714 us; the launch traced here: 707 us
  waiting for transfers between devices  410 us (57%)
  matrix products  103 us (14%)
  local copies, waits for them, and re-layouts  61.4 us (9%)
  blocking collectives  49.2 us (7%)
  other arithmetic  39.9 us (6%)
  starting transfers between devices  21 us (3%)
  between operations  15.4 us (2%)
    reduce_scatter x1, waiting for transfers between devices, shards(): lax.psum_scatter(grad_up, 'sq', scatter_dimension=0, tiled=True)  118 us
    reduce_scatter x1, waiting for transfers between devices, shards(): lax.psum_scatter(grad_down, 'sq', scatter_dimension=0, tiled=True)  117 us
    psum x1, waiting for transfers between devices, shards(): lax.psum(shares_sq[1].astype(jnp.bfloat16), 'dp').astype(jnp.float32)  82 us
    reduce_scatter x1, waiting for transfers between devices, shards(): lax.psum_scatter(grad_qkv, 'sq', scatter_dimension=0, tiled=True)  67.4 us
    dot_general x4, matrix products, contract_rows(): lax.dot_general(left, right, (((0,), (0,)), ((), ())), preferred_element_...  31.6 us
    ppermute x7, waiting for transfers between devices, collect(): lax.ppermute(pieces[far - 1], axis, [(d, (d - 1) % ways) for d in range(w...  24.7 us
    unnamed x109, local copies, waits for them, and re-layouts  22.1 us
    ppermute x7, starting transfers between devices, collect(): lax.ppermute(pieces[far - 1], axis, [(d, (d - 1) % ways) for d in range(w...  20.4 us
  transfers between devices with their start and end apart: 16, of which 11 were waited for; matrix products, arithmetic and copies ran while one was open for 25% of the time, Pallas kernels for 0%

profile of v1, /device:TPU:0, one launch (start us, length us, event | category | flops | bytes accessed | tf_op | source)
XLA Modules:
  0.0 706.7 jit_solution(10757730638805886928)
XLA Ops:
  9.0 4.0 convolution_convert_fusion
  24.8 5.5 collective-permute-done.1
  42.0 4.6 collective-permute-done.3
  75.9 4.0 copy.63
  80.0 14.4 %while.45 = (s32[]{:T(128)}, f32[1,16,128]{2,1,0:T(8,128)S(1)}, f32[1,16,128]{2,1,0:T(8,128)S(1)}, f32[1,16,128,64]{2,3,1,0:T(8,128)S(1)}, s32[2]{0:T(128)S(1)},...) while((s32[]{:T(128)}, f32[1,16,128]{2,1,0:T(8,128)S(1)}, ...), condition=%wide.region_9.10_spmd, body=%wide.region_3.9_spmd.sunk | while | flops 282544640 | bytes 20628860 | solution.py:63
  83.9 6.1 conditional.8
  99.7 5.2 fusion.92
  104.9 7.8 %fusion.60 = bf16[128,4096]{1,0:T(8,128)(2,1)S(1)} fusion(f32[128,4096]{1,0:T(8,128)S(1)} %fusion.92, bf16[4096,1024]{1,0:T(8,128)(2,1)} %param.27, bf16[1,128,1024]{2,1,0:T(8,128)(2,1)S(1)} %copy-done.18), kind=kOutput, calls=%fused_computation.80 | convolution fusion | flops 1084227584 | bytes 11796480 | tf_op jit(solution)/shard_map/dot_general | solution.py:73
  130.5 15.0 %all_gather.24 = bf16[1,1024,16]{1,2,0:T(8,128)(2,1)S(1)} all-gather(bf16[1,128,16]{1,2,0:T(8,128)(2,1)S(1)} %bitcast_convert_fusion), channel_id=1, replica_groups=mesh['dp'=4,'sq'=8] {'sq'}, dimensions={1}, use_global_device_ids=true | all-gather | bytes 36864 | tf_op jit(solution)/shard_map/all_gather | solution.py:261
  146.1 7.7 %all_gather.22 = bf16[1,1024,16]{1,2,0:T(8,128)(2,1)S(1)} all-gather(bf16[1,128,16]{1,2,0:T(8,128)(2,1)S(1)} %get-tuple-element.1073), channel_id=1, replica_groups=mesh['dp'=4,'sq'=8] {'sq'}, dimensions={1}, use_global_device_ids=true | all-gather | bytes 36864 | tf_op jit(solution)/shard_map/all_gather | solution.py:258
  153.8 4.1 copy.69
  160.0 20.2 %while.46 = (s32[]{:T(128)}, f32[1,16,128,64]{2,3,1,0:T(8,128)}, s32[2]{0:T(128)}, s32[128]{0:T(128)}, s32[1,8]{1,0:T(1,128)}, /*index=5*/s32[1,128]{1,0:T(1,128...) while((s32[]{:T(128)}, f32[1,16,128,64]{2,3,1,0:T(8,128)}, ...), condition=%wide.region_17.18_spmd, body=%wide.region_13.17_spmd.sunk | while | flops 409285120 | bytes 17499484 | solution.py:63
  164.4 11.4 %conditional.9 = (f32[1,16,128,64]{2,3,1,0:T(8,128)}) conditional(s32[]{:T(128)} %convert_element_type.291, f32[1,16,128,64]{2,3,1,0:T(8,128)} %get-tuple-element.1438, (s32[]{:T(128)}, s32[512]{0:T(512)S(1)}, s32[128]{0:T(128)}, s32[1,512,8]{1,2,0:T(8,128)S(1)}, s32[1,128]{1,0:T(1,128)}, /*index=5*/bf16[2,1,512,1024]{2,3,1,0:T(8,128)(2,1)}, ...), branch_computations={%region_14.14_spmd, %region_15.16_spmd} | conditional | flops 409276416 | bytes 17476628 | solution.py:200
  170.6 5.2 fusion.23
  186.9 37.1 %while.47 = (s32[]{:T(128)}, f32[1,16,128,64]{2,3,1,0:T(8,128)S(1)}, f32[1,16,128,64]{2,3,1,0:T(8,128)}, s32[2]{0:T(128)S(1)}, s32[]{:T(128)}, /*index=5*/s32[1,...) while((s32[]{:T(128)}, ...), condition=%wide.region_22.23_spmd.clone.clone, body=%wide.region_18.22_spmd.clone.clone.sunk | while | flops 547828352 | bytes 28265440 | solution.py:63
  188.9 16.6 %conditional.10 = ((f32[1,16,128,64]{2,3,1,0:T(8,128)S(1)}, f32[1,16,128,64]{2,3,1,0:T(8,128)})) conditional(s32[]{:T(128)} %convert_element_type.293, (f32[1,16,128,64]{2,3,1,0:T(8,128)S(1)}, f32[1,16,128,64]{2,3,1,0:T(8,128)}) %tuple.151, (s32[]{:T(128)}, s32[]{:T(128)}, s32[512]{0:T(512)S(1)}, s32[1,128]{1,0:T(1,128)}, ...), branch_computations={%region_19.19_spmd, %region_20.21_spmd} | conditional | flops 547819648 | bytes 28242020 | solution.py:251
  195.1 6.2 fusion.42
  201.2 4.2 fusion.43
  207.4 16.6 %conditional.10 = ((f32[1,16,128,64]{2,3,1,0:T(8,128)S(1)}, f32[1,16,128,64]{2,3,1,0:T(8,128)})) conditional(s32[]{:T(128)} %convert_element_type.293, (f32[1,16,128,64]{2,3,1,0:T(8,128)S(1)}, f32[1,16,128,64]{2,3,1,0:T(8,128)}) %tuple.151, (s32[]{:T(128)}, s32[]{:T(128)}, s32[512]{0:T(512)S(1)}, s32[1,128]{1,0:T(1,128)}, ...), branch_computations={%region_19.19_spmd, %region_20.21_spmd} | conditional | flops 547819648 | bytes 28242020 | solution.py:251
  213.6 6.2 fusion.42
  219.8 4.2 fusion.43
  225.2 7.5 %fusion.72 = f32[1024,3072]{1,0:T(8,128)} fusion(bf16[128,1024]{0,1:T(8,128)(2,1)S(1)} %bitcast.234, bf16[128,1024]{0,1:T(8,128)(2,1)S(1)} %bitcast.236, bf16[128,1024]{0,1:T(8,128)(2,1)} %bitcast.232, bf16[1,128,1024]{2,1,0:T(8,128)(2,1)S(1)} %copy-done.4, f32[1024]{0:T(1024)S(1)} %copy-done.33, f32[128]{0:T(128)S(1)} %copy-done.38), kind=kOutput, calls=%fused_computation.111 | convolution fusion | flops 808189952 | bytes 13636096 | tf_op jit(solution)/shard_map/dot_general | solution.py:67
  233.9 11.3 %fusion.91 = f32[1024,4096]{1,0:T(8,128)} fusion(bf16[128,4096]{1,0:T(8,128)(2,1)S(1)} %copy-done.9, f32[128,1024]{1,0:T(8,128)S(1)} %get-tuple-element.1090, f32[1024]{0:T(1024)S(1)} %copy-done.32, f32[128]{0:T(128)S(1)} %copy-done.35), kind=kOutput, calls=%fused_computation.157 | convolution fusion | flops 1074135040 | bytes 18354688 | tf_op jit(solution)/shard_map/dot_general | solution.py:67
  247.4 8.9 %fusion.74 = f32[4096,1024]{1,0:T(8,128)} fusion(bf16[1,128,1024]{2,1,0:T(8,128)(2,1)S(1)} %copy-done.19, f32[128,4096]{1,0:T(8,128)S(1)} %copy-done.3), kind=kOutput, calls=%fused_computation.113 | convolution fusion | flops 1078460416 | bytes 19136512 | tf_op jit(solution)/shard_map/dot_general | solution.py:67
  258.1 67.4 %reduce-scatter.5.cloned.1.call-done = f32[128,3072]{1,0:T(8,128)} async-done(((f32[1024,3072]{1,0:T(8,128)}), f32[128,3072]{1,0:T(8,128)}) %reduce-scatter.5.cloned.1.call-update) | async-done | bytes 1572880 | tf_op jit(solution)/shard_map/reduce_scatter | solution.py:284
  327.9 117.6 %reduce-scatter.9.cloned.1.call-done = f32[128,4096]{1,0:T(8,128)} async-done(((f32[1024,4096]{1,0:T(8,128)}), f32[128,4096]{1,0:T(8,128)}) %reduce-scatter.9.cloned.1.call-update) | async-done | bytes 2097168 | tf_op jit(solution)/shard_map/reduce_scatter | solution.py:287
  448.2 117.3 %reduce-scatter.11.cloned.1.call-done = f32[512,1024]{1,0:T(8,128)} async-done(((f32[4096,1024]{1,0:T(8,128)}), f32[512,1024]{1,0:T(8,128)}) %reduce-scatter.11.cloned.1.call-update) | async-done | bytes 2097168 | tf_op jit(solution)/shard_map/reduce_scatter | solution.py:288
  569.5 5.7 fusion.62
  575.3 5.2 fusion.66
  580.4 14.1 %all-reduce.2 = (bf16[1024]{0:T(1024)(128)(2,1)S(1)}, bf16[1024]{0:T(1024)(128)(2,1)S(1)}) all-reduce(f32[1024]{0:T(1024)S(1)} %get-tuple-element.989, f32[1024]{0:T(1024)S(1)} %copy-done.36), channel_id=6, replica_groups=mesh['dp'=4,'sq'=8] {'sq'}, use_global_device_ids=true, to_apply=%region_25.26.clone | all-reduce | flops 2048 | bytes 12288
  594.7 12.4 %all-reduce.3 = (bf16[128]{0:T(256)(128)(2,1)S(1)}, bf16[128]{0:T(256)(128)(2,1)S(1)}) all-reduce(bf16[128]{0:T(256)(128)(2,1)S(1)} %dynamic-slice.7, bf16[128]{0:T(256)(128)(2,1)S(1)} %dynamic-slice.6), channel_id=1, replica_groups=mesh['dp'=4,'sq'=8] {'dp'}, use_global_device_ids=true, to_apply=%region_26.27 | all-reduce | flops 256 | bytes 1024 | tf_op jit(solution)/shard_map/psum | solution.py:291
  609.2 82.0 %all-reduce.7.cloned.1.call-done = (bf16[128,3072]{1,0:T(8,128)(2,1)}, bf16[128,1024]{1,0:T(8,128)(2,1)}, bf16[128,4096]{1,0:T(8,128)(2,1)}, bf16[512,1024]{1,0:T(8,128)(2,1)}) async-done(((bf16[128,3072]{1,0:T(8,128)(2,1)}, bf16[128,1024]{1,0:T(8,128)(2,1)}, bf16[128,4096]{1,0:T(8,128)(2,1)}, bf16[512,1024]{1,0:T(8,128)(2,1)}), (bf16[128,3072]{1,0:T(8,128)(2,1)}, bf16[128,1024]{1,0:T(8,128)(2,1)}, ...) | async-done | bytes 3145744 | tf_op jit(solution)/shard_map/psum | solution.py:292
  (266 shorter events, 151.2 us)
Async XLA Ops:
  7.2 90.9 %copy-start = (bf16[1024,1024]{1,0:T(8,128)(2,1)S(1)}, bf16[1024,1024]{1,0:T(8,128)(2,1)}, u32[]{:S(2)}) copy-start(bf16[1024,1024]{1,0:T(8,128)(2,1)} %param.24) | copy-start | bytes 6291460
  7.2 68.8 %all-gather.9.cloned.1.call-start = ((), (), s32[]{:S(2)}) async-start(), calls=%async_computation.8 | async-start | bytes 2359296 | tf_op jit(solution)/shard_map/all_gather | solution.py:141
  9.0 31.6 %copy-start.42 = (s32[1,8]{1,0:T(1,128)S(1)}, s32[1,8]{1,0:T(1,128)}, u32[]{:S(2)}) copy-start(s32[1,8]{1,0:T(1,128)} %param.28) | copy-start | bytes 100
  13.9 111.1 %all-gather.13.cloned.1.call-start = ((), (), s32[]{:S(2)}) async-start(), calls=%async_computation.10 | async-start | bytes 2359296 | tf_op jit(solution)/shard_map/all_gather | solution.py:256
  14.7 139.2 %all-gather.11.cloned.1.call-start = ((), (), s32[]{:S(2)}) async-start(), calls=%async_computation.9 | async-start | bytes 2359296 | tf_op jit(solution)/shard_map/all_gather | solution.py:207
  14.7 7.3 %collective-permute-start = (bf16[1,128,1024]{2,1,0:T(8,128)(2,1)S(1)}, bf16[1,128,1024]{2,1,0:T(8,128)(2,1)S(1)}, u32[]{:S(2)}, u32[]{:S(2)}) collective-permute-start(bf16[1,128,1024]{2,1,0:T(8,128)(2,1)S(1)} %get-tuple-element.1086), channel_id=1, source_target_pairs={{0,7},{1,0},{2,1},{3,2},{4,3},{5,4},{6,5},{7,6},{8,15},{9,8},{10,9... | collective-permute-start | bytes 786440 | tf_op jit(solution)/shard_map/ppermute | solution.py:18
  22.0 8.3 %collective-permute-start.1 = (bf16[1,128,1024]{2,1,0:T(8,128)(2,1)S(1)}, bf16[1,128,1024]{2,1,0:T(8,128)(2,1)S(1)}, u32[]{:S(2)}, u32[]{:S(2)}) collective-permute-start(bf16[1,128,1024]{2,1,0:T(8,128)(2,1)S(1)} %collective-permute-done), channel_id=1, source_target_pairs={{0,7},{1,0},{2,1},{3,2},{4,3},{5,4},{6,5},{7,6},{8,15},{9,8},{10,9... | collective-permute-start | bytes 786440 | tf_op jit(solution)/shard_map/ppermute | solution.py:18
  31.0 6.8 collective-permute-start.2
  37.8 13.1 %copy-start.28 = (bf16[1,128,1024]{2,1,0:T(8,128)(2,1)}, bf16[1,128,1024]{2,1,0:T(8,128)(2,1)S(1)}, u32[]{:S(2)}) copy-start(bf16[1,128,1024]{2,1,0:T(8,128)(2,1)S(1)} %collective-permute-done.2) | copy-start | bytes 786436
  37.8 8.8 %collective-permute-start.3 = (bf16[1,128,1024]{2,1,0:T(8,128)(2,1)S(1)}, bf16[1,128,1024]{2,1,0:T(8,128)(2,1)}, u32[]{:S(2)}, u32[]{:S(2)}) collective-permute-start(bf16[1,128,1024]{2,1,0:T(8,128)(2,1)S(1)} %collective-permute-done.2), channel_id=1, source_target_pairs={{0,7},{1,0},{2,1},{3,2},{4,3},{5,4},{6,5},{7,6},{8,15},{9,8},{10,9... | collective-permute-start | bytes 786440 | tf_op jit(solution)/shard_map/ppermute | solution.py:18
  40.6 141.5 %all-gather.15.cloned.1.call-start = ((), (), s32[]{:S(2)}) async-start(), calls=%async_computation.11 | async-start | bytes 2359296 | tf_op jit(solution)/shard_map/all_gather | solution.py:257
  46.5 7.2 %collective-permute-start.4 = (bf16[1,128,1024]{2,1,0:T(8,128)(2,1)}, bf16[1,128,1024]{2,1,0:T(8,128)(2,1)}, u32[]{:S(2)}, u32[]{:S(2)}) collective-permute-start(bf16[1,128,1024]{2,1,0:T(8,128)(2,1)} %collective-permute-done.3), channel_id=1, source_target_pairs={{0,7},{1,0},{2,1},{3,2},{4,3},{5,4},{6,5},{7,6},{8,15},{9,8},{10,9... | collective-permute-start | bytes 786440 | tf_op jit(solution)/shard_map/ppermute | solution.py:18
  52.0 16.4 %copy-start.27 = (bf16[1,128,1024]{2,1,0:T(8,128)(2,1)S(1)}, bf16[1,128,1024]{2,1,0:T(8,128)(2,1)}, u32[]{:S(2)}) copy-start(bf16[1,128,1024]{2,1,0:T(8,128)(2,1)} %copy-done.26) | copy-start | bytes 786436
  52.0 16.5 %copy-start.29 = (bf16[1,128,1024]{2,1,0:T(8,128)(2,1)S(1)}, bf16[1,128,1024]{2,1,0:T(8,128)(2,1)}, u32[]{:S(2)}) copy-start(bf16[1,128,1024]{2,1,0:T(8,128)(2,1)} %copy-done.28) | copy-start | bytes 786436
  53.7 8.0 %collective-permute-start.5 = (bf16[1,128,1024]{2,1,0:T(8,128)(2,1)}, bf16[1,128,1024]{2,1,0:T(8,128)(2,1)S(1)}, u32[]{:S(2)}, u32[]{:S(2)}) collective-permute-start(bf16[1,128,1024]{2,1,0:T(8,128)(2,1)} %collective-permute-done.4), channel_id=1, source_target_pairs={{0,7},{1,0},{2,1},{3,2},{4,3},{5,4},{6,5},{7,6},{8,15},{9,8},{10,9... | collective-permute-start | bytes 786440 | tf_op jit(solution)/shard_map/ppermute | solution.py:18
  61.7 6.6 collective-permute-start.6
  80.0 18.1 %copy-start.4 = (bf16[1,128,1024]{2,1,0:T(8,128)(2,1)S(1)}, bf16[1,128,1024]{2,1,0:T(8,128)(2,1)}, u32[]{:S(2)}) copy-start(bf16[1,128,1024]{2,1,0:T(8,128)(2,1)} %param.21) | copy-start | bytes 786436
  99.7 16.7 %copy-start.34 = (f32[128]{0:T(128)}, f32[128]{0:T(128)S(1)}, u32[]{:S(2)}) copy-start(f32[128]{0:T(128)S(1)} %fusion.88) | copy-start | bytes 1540
  99.7 13.1 %slice-start = ((s8[8388608]{0:T(1024)(128)(4,1)}), s8[4194304]{0:T(1024)(128)(4,1)S(1)}, s32[]{:S(2)}) async-start(s8[8388608]{0:T(1024)(128)(4,1)} %bitcast.214), calls=%async_computation.13 | async-start | bytes 8388608
  104.9 7.8 %copy-start.2 = (f32[128,4096]{1,0:T(8,128)}, f32[128,4096]{1,0:T(8,128)S(1)}, u32[]{:S(2)}) copy-start(f32[128,4096]{1,0:T(8,128)S(1)} %fusion.92) | copy-start | bytes 6291460
  104.9 7.8 %slice-start.1 = ((s8[8388608]{0:T(1024)(128)(4,1)}), s8[4194304]{0:T(1024)(128)(4,1)S(1)}, s32[]{:S(2)}) async-start(s8[8388608]{0:T(1024)(128)(4,1)} %bitcast.214), calls=%async_computation.14 | async-start | bytes 8388608
  119.1 137.2 %reduce-scatter.7.cloned.1.call-start = ((), (), s32[]{:S(2)}) async-start(), calls=%async_computation.5 | async-start | bytes 4718592 | tf_op jit(solution)/shard_map/reduce_scatter | solution.py:285
  123.1 202.4 %reduce-scatter.5.cloned.1.call-start = ((), (), s32[]{:S(2)}) async-start(), calls=%async_computation.4 | async-start | bytes 14155776 | tf_op jit(solution)/shard_map/reduce_scatter | solution.py:284
  186.9 38.3 %copy-start.33 = (f32[1024]{0:T(1024)S(1)}, f32[1024]{0:T(1024)}, u32[]{:S(2)}) copy-start(f32[1024]{0:T(1024)} %param.22) | copy-start | bytes 12292
  186.9 38.3 %copy-start.38 = (f32[128]{0:T(128)S(1)}, f32[128]{0:T(128)}, u32[]{:S(2)}) copy-start(f32[128]{0:T(128)} %copy-done.37) | copy-start | bytes 1540
  232.7 212.7 %reduce-scatter.9.cloned.1.call-start = ((), (), s32[]{:S(2)}) async-start(), calls=%async_computation.6 | async-start | bytes 18874368 | tf_op jit(solution)/shard_map/reduce_scatter | solution.py:287
  245.2 320.2 %reduce-scatter.11.cloned.1.call-start = ((), (), s32[]{:S(2)}) async-start(), calls=%async_computation.7 | async-start | bytes 18874368 | tf_op jit(solution)/shard_map/reduce_scatter | solution.py:288
  256.3 435.0 %all-reduce.7.cloned.1.call-start = ((), (), s32[]{:S(2)}) async-start(), calls=%async_computation.12 | async-start | bytes 6291456 | tf_op jit(solution)/shard_map/psum | solution.py:292
  327.9 240.3 %copy-start.43 = (u32[32]{0:T(128)S(1)}, u32[32]{0:T(128)}, u32[]{:S(2)}) copy-start(u32[32]{0:T(128)} %constant.187) | copy-start | bytes 388
  575.2 33.0 %copy-start.41 = (f32[128]{0:T(128)S(1)}, f32[128]{0:T(128)}, u32[]{:S(2)}) copy-start(f32[128]{0:T(128)} %copy-done.40) | copy-start | bytes 1540
  575.2 33.0 %copy-start.6 = (f32[128,1024]{1,0:T(8,128)S(1)}, f32[128,1024]{1,0:T(8,128)}, u32[]{:S(2)}) copy-start(f32[128,1024]{1,0:T(8,128)} %copy-done.5) | copy-start | bytes 1572868
  691.2 8.7 %copy-start.1 = (bf16[1024,1024]{1,0:T(8,128)(2,1)S(1)}, bf16[1024,1024]{1,0:T(8,128)(2,1)}, u32[]{:S(2)}) copy-start(bf16[1024,1024]{1,0:T(8,128)(2,1)} %param.24) | copy-start | bytes 6291460
  (32 other events, 120.7 us)
Sparse Core Ops, SparseCore 0:
  14.0 35.5 all-gather.8
  51.5 28.9 all-gather.12
  82.9 27.8 all-gather.10
  119.2 35.2 all-gather.14
  157.7 51.3 reduce-scatter.6
  232.8 92.6 reduce-scatter.4
  329.5 115.9 reduce-scatter.8
  449.4 115.9 reduce-scatter.10
  568.8 122.3 all-reduce.6
